TPU v7x, 32 devices: a whole 2x2x4 slice. The times are simulated.
32 devices in a mesh: req: 16 (over z, x, core), blk: 2 (over y).
Axes of the slice: x: 2, y: 2, z: 4, core: 2. Of those that a mesh axis runs over, the one named last changes fastest.
Arguments:
- queries: bfloat16 [32, 64, 2048], P('req', 'blk'), may hold values from -5 to 5
- cache_keys: bfloat16 [32, 1024, 2048], P('req', 'blk'), may hold values from -5 to 5
- cache_values: bfloat16 [32, 1024, 2048], P('req', 'blk'), may hold values from -6 to 6
- draft_keys: bfloat16 [32, 64, 2048], P('req', 'blk'), may hold values from -6 to 6
- draft_values: bfloat16 [32, 64, 2048], P('req', 'blk'), may hold values from -6 to 6
- parents: int32 [32, 64], P('req'), may hold values from -1 to 62, as said below
- lengths: int32 [32], P('req'), may hold values from 2 to 1024
- out_weight: bfloat16 [2048, 4096], P('req'), may hold values from -0.125 to 0.125
Outputs:
- mixed: bfloat16 [32, 64, 4096], P('req', 'blk')
Inputs may be any that keep to these rules, and one draw needn't show every extreme that they name: parents[r, t] is below t; parents[r, 0] = -1 marks the root, which follows the cache.
All inputs are finite; a program needn't handle non-finite values.
Results may differ from a plain program's by a relative error of at most 0.0054.
Values may be sent and summed in bfloat16 or wider, within the bound.
A program may use at most 128 MiB of HBM per device.

v0:
```python
import functools

import jax
import jax.numpy as jnp
from jax import lax
from jax.experimental import pallas as pl
from jax.experimental.pallas import tpu as pltpu
from jax.sharding import PartitionSpec as P

HEAD = 128
HEADS = 16
LOW = 4
PARTS = 4
CHUNK = 256
MESH = pl.DeviceIdType.MESH
NEG = -1e30
COEF = HEAD**-0.5 * 1.4426950408889634


def flip(value, bits):
    out = value
    bit = 1
    while bit <= bits:
        if bits & bit:
            out = out + bit - 2 * bit * ((value // bit) % 2)
        bit *= 2
    return out


def kernel(
    nreq, nblk,
    q_hbm, ck_hbm, cv_hbm, dk_hbm, dv_hbm, par_ref, len_ref, w_hbm,
    out_hbm,
    qbuf, kbuf, vbuf, dkbuf, dvbuf, vis, nsend, nrecv, stat, ssend, srecv, abuf, wbuf, obuf,
    kv_sem, d_sem, q_send, q_recv, n_send, n_recv, s_send, s_recv,
    wz_send, wx_send, wc_send, w_recv, a_send, a_recv, o_send, o_recv,
):
    batch, own, width = q_hbm.shape
    keys = ck_hbm.shape[1]
    tree = own * nblk
    rows_w, model = w_hbm.shape
    group = 2 * nblk
    ncols = model // group
    depth = nreq // LOW
    req, blk = lax.axis_index("req"), lax.axis_index("blk")
    z, x, c = req // LOW, (req // 2) % 2, req % 2

    def at(zz, xx, cc):
        return zz * LOW + xx * 2 + cc

    part = width // PARTS
    pcols = [pl.ds(p * part, part) for p in range(PARTS)]

    locals_d = [
        pltpu.make_async_copy(q_hbm, qbuf.at[blk], d_sem.at[0]),
        pltpu.make_async_copy(dk_hbm, dkbuf, d_sem.at[1]),
        pltpu.make_async_copy(dv_hbm, dvbuf, d_sem.at[2]),
    ]
    for copy in locals_d:
        copy.start()
    kv = []
    for p in range(PARTS):
        pair = (
            pltpu.make_async_copy(ck_hbm.at[:, :, pcols[p]], kbuf.at[:, :, pcols[p]], kv_sem.at[0, p]),
            pltpu.make_async_copy(cv_hbm.at[:, :, pcols[p]], vbuf.at[:, :, pcols[p]], kv_sem.at[1, p]),
        )
        for copy in pair:
            copy.start()
        kv.append(pair)

    xpeer, cpeer = at(z, 1 - x, c), at(z, x, 1 - c)
    members = [
        (flip(z, a), lax.rem(blk + b, nblk)) for a in range(2) for b in range(nblk) if a or b
    ]
    peers = [(at(flip(z, d), x, c), blk) for d in range(1, depth)] + [(xpeer, blk), (cpeer, blk)]
    peers += [
        (at(flip(z, a), x, c), lax.rem(blk + b, nblk)) for a in range(2) for b in range(1, nblk)
    ]
    barrier = pltpu.get_barrier_semaphore()
    for peer in peers:
        pl.semaphore_signal(barrier, inc=1, device_id=peer, device_id_type=MESH)
    pl.semaphore_wait(barrier, len(peers))

    def remote(src, dst, send, recv, peer):
        return pltpu.make_async_remote_copy(
            src_ref=src, dst_ref=dst, send_sem=send, recv_sem=recv, device_id=peer, device_id_type=MESH
        )

    sent = []

    def send(*what):
        copy = remote(*what)
        copy.start()
        sent.append(copy)

    def await_recv(dst, sem):
        remote(dst, dst, wz_send.at[0], sem, (xpeer, blk)).wait_recv()

    for p in range(PARTS):
        for b in range(1, nblk):
            send(
                q_hbm.at[:, :, pcols[p]], qbuf.at[blk, :, :, pcols[p]],
                q_send.at[p, b], q_recv.at[p, blk], (req, lax.rem(blk + b, nblk)),
            )

    def wrows(source):
        return wbuf.at[pl.ds(pl.multiple_of(source * rows_w, rows_w), rows_w)]

    def wsrc(zz):
        index = (zz % 2) * nblk + blk
        return w_hbm.at[:, pl.ds(pl.multiple_of(index * ncols, ncols), ncols)]

    for d in range(1, depth):
        zz = flip(z, d)
        send(wsrc(zz), wrows(req), wz_send.at[d], w_recv.at[req], (at(zz, x, c), blk))
    send(wsrc(z), wrows(req), wx_send.at[0], w_recv.at[req], (xpeer, blk))
    send(wsrc(z), wrows(req), wc_send.at[0], w_recv.at[req], (cpeer, blk))
    own_w = pltpu.make_async_copy(wsrc(z), wrows(req), w_recv.at[req])
    own_w.start()

    def forward_z(d):
        source = at(flip(z, d), x, c)
        await_recv(wrows(source), w_recv.at[source])
        send(wrows(source), wrows(source), wx_send.at[d], w_recv.at[source], (xpeer, blk))
        send(wrows(source), wrows(source), wc_send.at[d], w_recv.at[source], (cpeer, blk))

    def forward_x(d):
        source = at(flip(z, d), 1 - x, c)
        await_recv(wrows(source), w_recv.at[source])
        send(wrows(source), wrows(source), wc_send.at[depth + d], w_recv.at[source], (cpeer, blk))

    row_i = lax.broadcasted_iota(jnp.int32, (tree, tree), 0)
    col_i = lax.broadcasted_iota(jnp.int32, (tree, tree), 1)
    pick = (
        lax.broadcasted_iota(jnp.int32, (tree, own), 0)
        == lax.broadcasted_iota(jnp.int32, (tree, own), 1) + blk * own
    ).astype(jnp.float32).astype(jnp.bfloat16)
    for r in range(batch):
        links = ((par_ref[pl.ds(r, 1), :] == row_i) | (row_i == col_i)).astype(jnp.float32)
        for _ in range((tree - 1).bit_length()):
            half = links.astype(jnp.bfloat16)
            links = jnp.minimum(jnp.dot(half, half, preferred_element_type=jnp.float32), 1.0)
        vis[r] = lax.dot_general(
            links.astype(jnp.bfloat16), pick, (((0,), (0,)), ((), ())),
            preferred_element_type=jnp.float32,
        )
    stat[...] = jnp.zeros_like(stat)

    slot = lax.broadcasted_iota(jnp.int32, (1, keys), 1) + blk * keys
    seen = [slot < len_ref[r] for r in range(batch)]
    lane = lax.broadcasted_iota(jnp.int32, (batch * own, 128), 1)
    per_p = HEADS // PARTS

    def head(p, h):
        cols = pl.ds(pl.multiple_of(h * HEAD, HEAD), HEAD)
        stats = []
        for r in range(batch):
            pieces = [qbuf[b, r, :, cols] for b in range(nblk)]
            if own % 16:
                q = jnp.concatenate([piece.astype(jnp.float32) for piece in pieces], axis=0)
                q = q.astype(jnp.bfloat16)
            else:
                q = jnp.concatenate(pieces, axis=0)
            dims = (((1,), (1,)), ((), ()))
            s1 = lax.dot_general(q, kbuf[r, :, cols], dims, preferred_element_type=jnp.float32)
            s2 = lax.dot_general(q, dkbuf[r, :, cols], dims, preferred_element_type=jnp.float32)
            s1 = jnp.where(seen[r], s1, NEG)
            s2 = jnp.where(vis[r] > 0.5, s2, NEG)
            top = jnp.maximum(
                jnp.max(s1, axis=-1, keepdims=True), jnp.max(s2, axis=-1, keepdims=True)
            )
            top = jnp.maximum(top, 0.1 * NEG)
            p1 = jnp.exp2((s1 - top) * COEF)
            p2 = jnp.exp2((s2 - top) * COEF)
            total = jnp.sum(p1, axis=-1, keepdims=True) + jnp.sum(p2, axis=-1, keepdims=True)
            numer = jnp.dot(
                p1.astype(jnp.bfloat16), vbuf[r, :, cols], preferred_element_type=jnp.float32
            ) + jnp.dot(
                p2.astype(jnp.bfloat16), dvbuf[r, :, cols], preferred_element_type=jnp.float32
            )
            stats.append((top, total, numer))
        at_lane = h - p * per_p
        for b in range(nblk):
            rows = slice(b * own, (b + 1) * own)
            top, total, numer = (
                jnp.concatenate([s[i][rows] for s in stats], axis=0) for i in range(3)
            )
            nsend[b, :, cols] = numer.astype(jnp.bfloat16)
            at_rows = pl.ds(b * batch * own, batch * own)
            stat[p, at_rows] = jnp.where(
                lane == at_lane, top, jnp.where(lane == at_lane + per_p, total, stat[p, at_rows])
            )

    def attend(p):
        for copy in kv[p]:
            copy.wait()
        for b in range(1, nblk):
            source = lax.rem(blk + b, nblk)
            await_recv(qbuf.at[source, :, :, pcols[p]], q_recv.at[p, source])

        def body(i, carry):
            head(p, p * per_p + 2 * i)
            head(p, p * per_p + 2 * i + 1)
            return carry

        lax.fori_loop(0, per_p // 2, body, 0)

    def exchange(p):
        ssend[p] = stat[p].T[: 2 * per_p]
        for b in range(1, nblk):
            to = (req, lax.rem(blk + b, nblk))
            send(
                nsend.at[:, :, pcols[p]], nrecv.at[blk, :, :, pcols[p]],
                n_send.at[p, b], n_recv.at[p, blk], to,
            )
            send(ssend.at[p], srecv.at[p, blk], s_send.at[p, b], s_recv.at[p, blk], to)

    zmod = z % 2
    mine = zmod * nblk + blk
    zpeer = (at(flip(z, 1), x, c), blk)

    def tokens(of):
        return abuf.at[pl.ds(of * nblk, nblk)]

    def merge(p):
        stats = [stat[p][:, : 2 * per_p]]
        for b in range(1, nblk):
            source = lax.rem(blk + b, nblk)
            await_recv(nrecv.at[source, :, :, pcols[p]], n_recv.at[p, source])
            await_recv(srecv.at[p, source], s_recv.at[p, source])
            stats.append(srecv[p, source].T)
        tops = [s[:, :per_p] for s in stats]
        sums = [s[:, per_p:] for s in stats]
        top = functools.reduce(jnp.maximum, tops)
        factors = [jnp.exp2((t - top) * COEF) for t in tops]
        total = sum(s * f for s, f in zip(sums, factors))
        factors = [f / total for f in factors]
        for b in range(nblk):
            rows = slice(b * batch * own, (b + 1) * batch * own)
            for i in range(per_p):
                cols = pl.ds((p * per_p + i) * HEAD, HEAD)
                row = nsend[b, :, cols].astype(jnp.float32) * factors[0][rows, i : i + 1]
                for a in range(1, nblk):
                    piece = nrecv[lax.rem(blk + a, nblk), b, :, cols].astype(jnp.float32)
                    row = row + piece * factors[a][rows, i : i + 1]
                abuf[zmod * nblk + b, :, cols] = row.astype(jnp.bfloat16)
        block = tokens(zmod).at[:, :, pcols[p]]
        send(block, block, a_send.at[p], a_recv.at[p], zpeer)

    for copy in locals_d:
        copy.wait()

    attend(0)
    exchange(0)
    attend(1)
    exchange(1)
    forward_z(1)
    forward_x(0)
    merge(0)
    attend(2)
    exchange(2)
    forward_z(2)
    forward_x(1)
    merge(1)
    attend(3)
    exchange(3)
    for d in range(3, depth):
        forward_z(d)
    merge(2)
    merge(3)
    for d in range(2, depth):
        forward_x(d)

    own_w.wait()
    for source in range(depth):
        for low in ((x, 1 - c), (1 - x, 1 - c)):
            index = at(flip(z, source), *low)
            await_recv(wrows(index), w_recv.at[index])
    for p in range(PARTS):
        await_recv(tokens(1 - zmod).at[:, :, pcols[p]], a_recv.at[p])

    homes = []
    for n in range(ncols // CHUNK):
        cols = pl.ds(n * CHUNK, CHUNK)
        mixed = jnp.dot(
            abuf[...].reshape(group * batch * own, width), wbuf[:, cols],
            preferred_element_type=jnp.float32,
        )
        obuf[:, :, :, cols] = mixed.reshape(group, batch, own, CHUNK).astype(jnp.bfloat16)
        there = pl.ds(pl.multiple_of(mine * ncols + n * CHUNK, CHUNK), CHUNK)
        for j, (zz, yy) in enumerate(members):
            index = (zz % 2) * nblk + yy
            send(
                obuf.at[index, :, :, cols], out_hbm.at[:, :, there],
                o_send.at[n, j], o_recv.at[n, mine], (at(zz, x, c), yy),
            )
        home = pltpu.make_async_copy(obuf.at[mine, :, :, cols], out_hbm.at[:, :, there], o_recv.at[n, mine])
        home.start()
        homes.append(home)
    for n in range(ncols // CHUNK):
        homes[n].wait()
        for zz, yy in members:
            index = (zz % 2) * nblk + yy
            there = pl.ds(pl.multiple_of(index * ncols + n * CHUNK, CHUNK), CHUNK)
            await_recv(out_hbm.at[:, :, there], o_recv.at[n, index])
    for copy in sent:
        copy.wait_send()


def shards(nreq, nblk, queries, cache_keys, cache_values, draft_keys, draft_values, parents, lengths, out_weight):
    batch, own, width = queries.shape
    keys = cache_keys.shape[1]
    tree = own * nblk
    rows_w, model = out_weight.shape
    group = 2 * nblk
    ncols = model // group
    depth = nreq // LOW
    bf16, f32 = jnp.bfloat16, jnp.float32
    dma = pltpu.SemaphoreType.DMA
    hbm = pl.BlockSpec(memory_space=pltpu.HBM)
    vmem = pl.BlockSpec(memory_space=pltpu.VMEM)
    smem = pl.BlockSpec(memory_space=pltpu.SMEM)
    pieces = ncols // CHUNK
    return pl.pallas_call(
        functools.partial(kernel, nreq, nblk),
        out_shape=jax.ShapeDtypeStruct((batch, own, model), bf16),
        in_specs=[hbm, hbm, hbm, hbm, hbm, vmem, smem, hbm],
        out_specs=hbm,
        scratch_shapes=[
            pltpu.VMEM((nblk, batch, own, width), bf16),
            pltpu.VMEM((batch, keys, width), bf16),
            pltpu.VMEM((batch, keys, width), bf16),
            pltpu.VMEM((batch, own, width), bf16),
            pltpu.VMEM((batch, own, width), bf16),
            pltpu.VMEM((batch, tree, own), f32),
            pltpu.VMEM((nblk, batch * own, width), bf16),
            pltpu.VMEM((nblk, nblk, batch * own, width), bf16),
            pltpu.VMEM((PARTS, batch * tree, 128), f32),
            pltpu.VMEM((PARTS, 2 * HEADS // PARTS, batch * tree), f32),
            pltpu.VMEM((PARTS, nblk, 2 * HEADS // PARTS, batch * tree), f32),
            pltpu.VMEM((group, batch * own, width), bf16),
            pltpu.VMEM((rows_w * nreq, ncols), bf16),
            pltpu.VMEM((group, batch, own, ncols), bf16),
            dma((2, PARTS)),
            dma((3,)),
            dma((PARTS, nblk)),
            dma((PARTS, nblk)),
            dma((PARTS, nblk)),
            dma((PARTS, nblk)),
            dma((PARTS, nblk)),
            dma((PARTS, nblk)),
            dma((depth,)),
            dma((depth,)),
            dma((2 * depth,)),
            dma((nreq,)),
            dma((PARTS,)),
            dma((PARTS,)),
            dma((pieces, group)),
            dma((pieces, group)),
        ],
        compiler_params=pltpu.CompilerParams(
            collective_id=0, has_side_effects=True, vmem_limit_bytes=58 * 1024 * 1024
        ),
    )(queries, cache_keys, cache_values, draft_keys, draft_values, parents, lengths, out_weight)


def solution(mesh):
    in_specs = (
        P("req", "blk", None),
        P("req", "blk", None),
        P("req", "blk", None),
        P("req", "blk", None),
        P("req", "blk", None),
        P("req", None),
        P("req"),
        P("req", None),
    )
    out_specs = P("req", "blk", None)
    body = functools.partial(shards, mesh.shape["req"], mesh.shape["blk"])
    return jax.shard_map(body, mesh=mesh, in_specs=in_specs, out_specs=out_specs, check_vma=False)
```

profile of v0, /device:TPU:1, one launch (start us, length us, event | category | flops | bytes accessed | tf_op | source)
XLA Modules:
  0.0 49.3 jit_solution(18433656316005817359)
XLA Ops:
  0.0 47.4 %shard_map.82 = bf16[2,32,4096]{2,1,0:T(8,128)(2,1)} custom-call(bf16[2,32,2048]{2,1,0:T(8,128)(2,1)} %q_hbm.1, bf16[2,512,2048]{2,1,0:T(8,128)(2,1)} %ck_hbm.1, bf16[2,512,2048]{2,1,0:T(8,128)(2,1)} %cv_hbm.1, bf16[2,32,2048]{2,1,0:T(8,128)(2,1)} %dk_hbm.1, bf16[2,32,2048]{2,1,0:T(8,128)(2,1)} %dv_hbm.1, s32[2,64]{1,0:T(2,128)} %par_ref.1, s32[2]{0:T(128)} %len_ref.1, ...), custom_call_target="tpu_custom_call" | custom-call | tf_op jit(solution)/shard_map/pallas_call | solution.py:324
  47.4 1.9 %copy.10 = bf16[2,32,4096]{2,1,0:T(8,128)(2,1)} copy(bf16[2,32,4096]{2,1,0:T(8,128)(2,1)} %shard_map.82) | data formatting | bytes 1048576
where the time goes:
time: 50.2 us; the launch traced here: 49.3 us
  Pallas kernels  47.4 us (94%)
  local copies, waits for them, and re-layouts  1.87 us (4%)
    pallas_call x1, Pallas kernels, shards(): pl.pallas_call(functools.partial(kernel, nreq, nblk), out_shape=jax.Shape...  47.4 us
    unnamed x1, local copies, waits for them, and re-layouts  1.87 us

commit v1 on v0

v1 whole, which is shorter than its diff:
```python
import functools

import jax
import jax.numpy as jnp
from jax import lax
from jax.experimental import pallas as pl
from jax.experimental.pallas import tpu as pltpu
from jax.sharding import PartitionSpec as P

HEAD = 128
HEADS = 16
LOW = 4
PARTS = 4
CHUNK = 256
FIRST = 14
NEAR = 2
ORDER = ((0, 1), (1, 1), (0, 2), (0, 3), (1, 2), (1, 3), )
STEPS = ((0, 1), (1, 1), (0, 2), (0, 3), (1, 2), (1, 3), )
PASSED = (0, 1, )
SCHEDULE = ("a00", "w", "w", "a01", "e0", "w", "w", "a10", "a11", "e1", "w", "w", "m0", "a20", "a21", "e2", "m1", "w", "a30", "a31", "e3", "w", "m2", "z0", "w", "m3", "w", "f0", "z1", "w", "w", "w", "f1", "z2", "w", "z3", "p00", "p01", "p10", "p11",)
MESH = pl.DeviceIdType.MESH
NEG = -1e30
COEF = HEAD**-0.5 * 1.4426950408889634


def flip(value, bits):
    out = value
    bit = 1
    while bit <= bits:
        if bits & bit:
            out = out + bit - 2 * bit * ((value // bit) % 2)
        bit *= 2
    return out


def kernel(
    nreq, nblk,
    q_hbm, ck_hbm, cv_hbm, dk_hbm, dv_hbm, par_ref, len_ref, w_hbm,
    out_hbm,
    qbuf, kbuf, vbuf, dkbuf, dvbuf, vtmp, vis, nown, nsend, nrecv, stat, ssend, srecv, abuf, wbuf, obuf,
    kv_sem, d_sem, q_send, q_recv, n_send, n_recv, s_send, s_recv,
    wz_send, wx_send, w_recv, known, a_send, a_recv, o_send, o_recv,
):
    batch, own, width = q_hbm.shape
    keys = ck_hbm.shape[1]
    tree = own * nblk
    rows = batch * own
    rows_w, model = w_hbm.shape
    ncols = model // (4 * nblk)
    chunk = min(CHUNK, ncols)
    pieces = ncols // chunk
    depth = nreq // LOW
    req, blk = lax.axis_index("req"), lax.axis_index("blk")
    z, x, c = req // LOW, (req // 2) % 2, req % 2

    def at(zz, xx, cc):
        return zz * LOW + xx * 2 + cc

    def slot(zr, cr, yr):
        return (zr * 2 + cr) * nblk + yr

    def member(zr, cr, yr):
        return (at(flip(z, zr), x, flip(c, cr)), lax.rem(blk + yr, nblk))

    def columns(zz, yy, cc, n):
        index = ((zz % 2) * nblk + yy) * 2 + cc
        return pl.ds(pl.multiple_of(index * ncols + n * chunk, chunk), chunk)

    def back(yr):
        return (nblk - yr) % nblk

    part = width // PARTS
    pcols = [pl.ds(p * part, part) for p in range(PARTS)]

    locals_d = [
        pltpu.make_async_copy(q_hbm, qbuf.at[0], d_sem.at[0]),
        pltpu.make_async_copy(dk_hbm, dkbuf, d_sem.at[1]),
        pltpu.make_async_copy(dv_hbm, dvbuf, d_sem.at[2]),
    ]
    for copy in locals_d:
        copy.start()
    kv = []
    for p in range(PARTS):
        pair = (
            pltpu.make_async_copy(ck_hbm.at[:, :, pcols[p]], kbuf.at[:, :, pcols[p]], kv_sem.at[0, p]),
            pltpu.make_async_copy(cv_hbm.at[:, :, pcols[p]], vbuf.at[:, :, pcols[p]], kv_sem.at[1, p]),
        )
        for copy in pair:
            copy.start()
        kv.append(pair)

    xpeer = (at(z, 1 - x, c), blk)
    line = [(d, e) for d in range(depth) for e in range(2) if d or e]
    peers = [xpeer, (at(z, x, 1 - c), blk)] + [member(0, 0, b) for b in range(1, nblk)]
    barrier = pltpu.get_barrier_semaphore()

    def beside(act):
        for side, exists in ((z - 1, z > 0), (z + 1, z < depth - 1)):
            @pl.when(exists)
            def _():
                act(side)

    ends = (z == 0).astype(jnp.int32) + (z == depth - 1).astype(jnp.int32)
    for peer in peers:
        pl.semaphore_signal(barrier, inc=1, device_id=peer, device_id_type=MESH)

    def greet(side):
        for cc in range(2):
            pl.semaphore_signal(barrier, inc=1, device_id=(at(side, x, cc), blk), device_id_type=MESH)

    beside(greet)
    pl.semaphore_wait(barrier, len(peers) + 4 - 2 * ends)

    def tell(s):
        def signal(side):
            pl.semaphore_signal(known.at[s], inc=1, device_id=(at(side, x, c), blk), device_id_type=MESH)

        beside(signal)

    def stage(s):
        pl.semaphore_wait(known.at[s], 2 - ends)
        if s + 1 < depth - 2:
            tell(s + 1)

    def remote(src, dst, send, recv, peer):
        return pltpu.make_async_remote_copy(
            src_ref=src, dst_ref=dst, send_sem=send, recv_sem=recv, device_id=peer, device_id_type=MESH
        )

    sent = []

    def send(*what):
        copy = remote(*what)
        copy.start()
        sent.append(copy)

    def await_recv(dst, sem):
        remote(dst, dst, wx_send.at[0, 0, 0], sem, xpeer).wait_recv()

    for p in range(PARTS):
        for b in range(1, nblk):
            send(
                q_hbm.at[:, :, pcols[p]], qbuf.at[back(b), :, :, pcols[p]],
                q_send.at[p, b], q_recv.at[p, back(b)], member(0, 0, b),
            )

    def wdst(n, source):
        return wbuf.at[pl.ds(pl.multiple_of(source * rows_w, rows_w), rows_w), pl.ds(n * chunk, chunk)]

    def wsrc(n, zz, cc):
        return w_hbm.at[:, columns(zz, blk, cc, n)]

    own_w = []
    for n in range(pieces):
        send(wsrc(n, z, c), wdst(n, req), wx_send.at[n, 0, 0], w_recv.at[n, req], xpeer)
        copy = pltpu.make_async_copy(wsrc(n, z, c), wdst(n, req), w_recv.at[n, req])
        copy.start()
        own_w.append(copy)

    rest = [(n, d) for n, d in ORDER if n < pieces and d < depth]
    rest += [(n, d) for n in range(pieces) for d in range(1, depth) if (n, d) not in rest]
    puts = [(n, 0, 1) for n in range(pieces)] + [(n, d, e) for n, d in rest for e in range(2)]
    order = [(n, d) for n, d in STEPS if n < pieces and d < depth]
    order += [pair for pair in rest if pair not in order]
    steps = [(n, 0, 1) for n in range(pieces)] + [(n, d, e) for n, d in order for e in range(2)]
    done, gone = [0], [0]

    def pump(upto):
        while gone[0] < min(upto, len(puts)):
            n, d, e = puts[gone[0]]
            gone[0] += 1
            zz, cc = flip(z, d), flip(c, e)
            send(wsrc(n, zz, cc), wdst(n, req), wz_send.at[n, d, e], w_recv.at[n, req], (at(zz, x, cc), blk))

    pump(pieces + 2 * sum(d == 1 for _, d in rest[:NEAR]))
    if depth > 2:
        tell(0)

    def forward(upto):
        while done[0] < min(upto, len(steps)):
            n, d, e = steps[done[0]]
            done[0] += 1
            source = at(flip(z, d), x, flip(c, e))
            await_recv(wdst(n, source), w_recv.at[n, source])
            send(wdst(n, source), wdst(n, source), wx_send.at[n, d, e], w_recv.at[n, source], xpeer)

    row_i = lax.broadcasted_iota(jnp.int32, (tree, tree), 0)
    col_i = lax.broadcasted_iota(jnp.int32, (tree, tree), 1)
    pick = (
        lax.broadcasted_iota(jnp.int32, (tree, own), 0)
        == lax.broadcasted_iota(jnp.int32, (tree, own), 1) + blk * own
    ).astype(jnp.float32).astype(jnp.bfloat16)
    for r in range(batch):
        links = ((par_ref[pl.ds(r, 1), :] == row_i) | (row_i == col_i)).astype(jnp.float32)
        for _ in range((tree - 1).bit_length()):
            half = links.astype(jnp.bfloat16)
            links = jnp.minimum(jnp.dot(half, half, preferred_element_type=jnp.float32), 1.0)
        vtmp[r] = lax.dot_general(
            links.astype(jnp.bfloat16), pick, (((0,), (0,)), ((), ())),
            preferred_element_type=jnp.float32,
        )
    for r in range(batch):
        for b in range(nblk):
            there = pl.ds(pl.multiple_of(lax.rem(blk + b, nblk) * own, own), own)
            vis[r, pl.ds(b * own, own)] = vtmp[r, there]
    stat[...] = jnp.zeros_like(stat)
    for s in range(depth - 2):
        stage(s)
    pump(FIRST)

    at_key = lax.broadcasted_iota(jnp.int32, (1, keys), 1) + blk * keys
    seen = [at_key < len_ref[r] for r in range(batch)]
    lane = lax.broadcasted_iota(jnp.int32, (rows, 128), 1)
    per_p = HEADS // PARTS

    def head(p, i):
        cols = pl.ds((p * per_p + i) * HEAD, HEAD)
        stats = []
        for r in range(batch):
            tokens = [qbuf[b, r, :, cols] for b in range(nblk)]
            if own % 16:
                q = jnp.concatenate([piece.astype(jnp.float32) for piece in tokens], axis=0)
                q = q.astype(jnp.bfloat16)
            else:
                q = jnp.concatenate(tokens, axis=0)
            dims = (((1,), (1,)), ((), ()))
            s1 = lax.dot_general(q, kbuf[r, :, cols], dims, preferred_element_type=jnp.float32)
            s2 = lax.dot_general(q, dkbuf[r, :, cols], dims, preferred_element_type=jnp.float32)
            s1 = jnp.where(seen[r], s1, NEG)
            s2 = jnp.where(vis[r] > 0.5, s2, NEG)
            top = jnp.maximum(
                jnp.max(s1, axis=-1, keepdims=True), jnp.max(s2, axis=-1, keepdims=True)
            )
            top = jnp.maximum(top, 0.1 * NEG)
            p1 = jnp.exp2((s1 - top) * COEF)
            p2 = jnp.exp2((s2 - top) * COEF)
            total = jnp.sum(p1, axis=-1, keepdims=True) + jnp.sum(p2, axis=-1, keepdims=True)
            numer = jnp.dot(
                p1.astype(jnp.bfloat16), vbuf[r, :, cols], preferred_element_type=jnp.float32
            ) + jnp.dot(
                p2.astype(jnp.bfloat16), dvbuf[r, :, cols], preferred_element_type=jnp.float32
            )
            stats.append((top, total, numer))
        for b in range(nblk):
            of = slice(b * own, (b + 1) * own)
            top, total, numer = (
                jnp.concatenate([s[j][of] for s in stats], axis=0) for j in range(3)
            )
            nown[b, :, cols] = numer
            nsend[b, :, cols] = numer.astype(jnp.bfloat16)
            at_rows = pl.ds(b * rows, rows)
            stat[p, at_rows] = jnp.where(
                lane == i, top, jnp.where(lane == i + per_p, total, stat[p, at_rows])
            )

    def attend(p, half):
        if half == 0:
            for copy in kv[p]:
                copy.wait()
            for b in range(1, nblk):
                await_recv(qbuf.at[b, :, :, pcols[p]], q_recv.at[p, b])
        for i in range(half * per_p // 2, (half + 1) * per_p // 2):
            head(p, i)

    def exchange(p):
        ssend[p] = stat[p].T[: 2 * per_p]
        for b in range(1, nblk):
            send(
                nsend.at[:, :, pcols[p]], nrecv.at[back(b), :, :, pcols[p]],
                n_send.at[p, b], n_recv.at[p, back(b)], member(0, 0, b),
            )
            send(ssend.at[p], srecv.at[p, back(b)], s_send.at[p, b], s_recv.at[p, back(b)], member(0, 0, b))

    def piece(zr, cr, yr, p):
        if yr is None:
            return abuf.at[pl.ds(slot(zr, cr, 0), nblk), :, pcols[p]]
        return abuf.at[slot(zr, cr, yr), :, pcols[p]]

    def sem(zr, cr, yr, p):
        return a_recv.at[p, slot(zr, cr, yr or 0)]

    def share(p, mine, there, to, s):
        send(piece(*mine, p), piece(*there, p), a_send.at[p, s], sem(*there, p), member(*to))

    def merge(p):
        stats = [stat[p]]
        for a in range(1, nblk):
            await_recv(nrecv.at[a, :, :, pcols[p]], n_recv.at[p, a])
            await_recv(srecv.at[p, a], s_recv.at[p, a])
            stats.append(srecv[p, a].T)
        for b in range(nblk):
            places = [(b - a) % nblk for a in range(nblk)]
            own_stats = [s[k * rows : (k + 1) * rows] for s, k in zip(stats, places)]
            tops = [s[:, :per_p] for s in own_stats]
            sums = [s[:, per_p : 2 * per_p] for s in own_stats]
            top = functools.reduce(jnp.maximum, tops)
            factors = [jnp.exp2((t - top) * COEF) for t in tops]
            total = sum(s * f for s, f in zip(sums, factors))
            factors = [f / total for f in factors]
            for i in range(per_p):
                cols = pl.ds((p * per_p + i) * HEAD, HEAD)
                row = nown[b, :, cols] * factors[0][:, i : i + 1]
                for a in range(1, nblk):
                    row = row + nrecv[a, places[a], :, cols].astype(jnp.float32) * factors[a][:, i : i + 1]
                abuf[b, :, cols] = row.astype(jnp.bfloat16)
            if b == 0 and p in PASSED:
                share(p, (0, 0, 0), (1, 0, 0), (1, 0, 0), 0)
        if p not in PASSED:
            share(p, (0, 0, None), (1, 0, None), (1, 0, 0), 0)
        share(p, (0, 0, None), (0, 1, None), (0, 1, 0), 1)

    def near(p):
        yr = 0 if p in PASSED else None
        await_recv(piece(1, 0, yr, p), sem(1, 0, yr, p))
        if p in PASSED:
            for b in range(1, nblk):
                share(p, (1, 0, 0), (1, 0, back(b)), (0, 0, b), 2 + b)
        share(p, (1, 0, yr), (1, 1, yr), (0, 1, 0), 2)

    def far(p):
        if p in PASSED:
            for b in range(1, nblk):
                await_recv(piece(1, 0, b, p), sem(1, 0, b, p))
                share(p, (1, 0, b), (1, 1, b), (0, 1, 0), 2 + nblk + b)

    for copy in locals_d:
        copy.wait()

    ymembers = [(cr, yr) for cr in range(2) for yr in range(nblk)]

    def project(n, zr):
        cols = pl.ds(n * chunk, chunk)
        out = jnp.dot(
            abuf[pl.ds(zr * 2 * nblk, 2 * nblk)].reshape(2 * nblk * rows, width), wbuf[:, cols],
            preferred_element_type=jnp.float32,
        )
        obuf[pl.ds(zr * 2 * nblk, 2 * nblk), :, :, cols] = out.reshape(2 * nblk, batch, own, chunk).astype(jnp.bfloat16)
        there = columns(z, blk, c, n)
        for cr, yr in ymembers:
            k = slot(zr, cr, yr)
            if k:
                to = slot(zr, cr, back(yr))
                send(
                    obuf.at[k, :, :, cols], out_hbm.at[:, :, there],
                    o_send.at[n, k], o_recv.at[n, to], member(zr, cr, yr),
                )
            else:
                home = pltpu.make_async_copy(obuf.at[0, :, :, cols], out_hbm.at[:, :, there], o_recv.at[n, 0])
                home.start()
                homes.append(home)

    homes = []
    ready = set()

    def finish(n, zr):
        if n >= pieces:
            return
        if zr == 0:
            pump(len(puts))
            forward(1 + max(k for k, step in enumerate(steps) if step[0] == n))
            own_w[n].wait()
            for d in range(depth):
                for e in range(2):
                    source = at(flip(z, d), 1 - x, flip(c, e))
                    await_recv(wdst(n, source), w_recv.at[n, source])
        if n == 0:
            for p in range(PARTS):
                for yr in range(nblk) if zr and p in PASSED else (None,):
                    await_recv(piece(zr, 1, yr, p), sem(zr, 1, yr, p))
        project(n, zr)

    for op in SCHEDULE:
        kind, a, b = op[0], int(op[1:] or 0), int(op[-1:] if op[1:] else 0)
        if kind == "a":
            attend(a // 10, b)
        elif kind == "e":
            exchange(a)
        elif kind == "m":
            merge(a)
        elif kind == "z":
            near(a)
        elif kind == "f":
            far(a)
        elif kind == "s":
            pump(gone[0] + 1)
        elif kind == "w":
            forward(done[0] + 1)
        else:
            finish(a // 10, b)
    for n in range(pieces):
        homes[n].wait()
        for zr in range(2):
            for cr, yr in ymembers:
                k = slot(zr, cr, yr)
                if k:
                    there = columns(flip(z, zr), lax.rem(blk + yr, nblk), flip(c, cr), n)
                    await_recv(out_hbm.at[:, :, there], o_recv.at[n, k])
    for copy in sent:
        copy.wait_send()


def shards(nreq, nblk, queries, cache_keys, cache_values, draft_keys, draft_values, parents, lengths, out_weight):
    batch, own, width = queries.shape
    keys = cache_keys.shape[1]
    tree = own * nblk
    rows = batch * own
    rows_w, model = out_weight.shape
    group = 4 * nblk
    ncols = model // group
    pieces = ncols // min(CHUNK, ncols)
    depth = nreq // LOW
    bf16, f32 = jnp.bfloat16, jnp.float32
    dma = pltpu.SemaphoreType.DMA
    hbm = pl.BlockSpec(memory_space=pltpu.HBM)
    vmem = pl.BlockSpec(memory_space=pltpu.VMEM)
    smem = pl.BlockSpec(memory_space=pltpu.SMEM)
    return pl.pallas_call(
        functools.partial(kernel, nreq, nblk),
        out_shape=jax.ShapeDtypeStruct((batch, own, model), bf16),
        in_specs=[hbm, hbm, hbm, hbm, hbm, vmem, smem, hbm],
        out_specs=hbm,
        scratch_shapes=[
            pltpu.VMEM((nblk, batch, own, width), bf16),
            pltpu.VMEM((batch, keys, width), bf16),
            pltpu.VMEM((batch, keys, width), bf16),
            pltpu.VMEM((batch, own, width), bf16),
            pltpu.VMEM((batch, own, width), bf16),
            pltpu.VMEM((batch, tree, own), f32),
            pltpu.VMEM((batch, tree, own), f32),
            pltpu.VMEM((nblk, rows, width), f32),
            pltpu.VMEM((nblk, rows, width), bf16),
            pltpu.VMEM((nblk, nblk, rows, width), bf16),
            pltpu.VMEM((PARTS, batch * tree, 128), f32),
            pltpu.VMEM((PARTS, 2 * HEADS // PARTS, batch * tree), f32),
            pltpu.VMEM((PARTS, nblk, 2 * HEADS // PARTS, batch * tree), f32),
            pltpu.VMEM((group, rows, width), bf16),
            pltpu.VMEM((rows_w * nreq, ncols), bf16),
            pltpu.VMEM((group, batch, own, ncols), bf16),
            dma((2, PARTS)),
            dma((3,)),
            dma((PARTS, nblk)),
            dma((PARTS, nblk)),
            dma((PARTS, nblk)),
            dma((PARTS, nblk)),
            dma((PARTS, nblk)),
            dma((PARTS, nblk)),
            dma((pieces, depth, 2)),
            dma((pieces, depth, 2)),
            dma((pieces, nreq)),
            pltpu.SemaphoreType.REGULAR((depth - 2,)),
            dma((PARTS, 2 + 4 * nblk)),
            dma((PARTS, group)),
            dma((pieces, group)),
            dma((pieces, group)),
        ],
        compiler_params=pltpu.CompilerParams(
            collective_id=0, has_side_effects=True, vmem_limit_bytes=58 * 1024 * 1024
        ),
    )(queries, cache_keys, cache_values, draft_keys, draft_values, parents, lengths, out_weight)


def solution(mesh):
    in_specs = (
        P("req", "blk", None),
        P("req", "blk", None),
        P("req", "blk", None),
        P("req", "blk", None),
        P("req", "blk", None),
        P("req", None),
        P("req"),
        P("req", None),
    )
    out_specs = P("req", "blk", None)
    body = functools.partial(shards, mesh.shape["req"], mesh.shape["blk"])
    return jax.shard_map(body, mesh=mesh, in_specs=in_specs, out_specs=out_specs, check_vma=False)
```

time: 50.2 us -> 46.5 us (0.926); the launches traced: 49.3 us -> 46.4 us
  Pallas kernels: 47.4 us -> 44.5 us
    pallas_call x1, Pallas kernels: 47.4 us -> 44.5 us  [shards(): pl.pallas_call(functools.partial(kernel, nreq, nblk), out_shape=jax.Shape...]
where the time goes in v1:
time: 46.5 us; the launch traced here: 46.4 us
  Pallas kernels  44.5 us (96%)
  local copies, waits for them, and re-layouts  1.87 us (4%)
    pallas_call x1, Pallas kernels, shards(): pl.pallas_call(functools.partial(kernel, nreq, nblk), out_shape=jax.Shape...  44.5 us
    unnamed x1, local copies, waits for them, and re-layouts  1.87 us

profile of v1, /device:TPU:1, one launch (start us, length us, event | category | flops | bytes accessed | tf_op | source)
XLA Modules:
  0.0 46.4 jit_solution(458736083086390912)
XLA Ops:
  0.0 44.5 %shard_map.82 = bf16[2,32,4096]{2,1,0:T(8,128)(2,1)} custom-call(bf16[2,32,2048]{2,1,0:T(8,128)(2,1)} %q_hbm.1, bf16[2,512,2048]{2,1,0:T(8,128)(2,1)} %ck_hbm.1, bf16[2,512,2048]{2,1,0:T(8,128)(2,1)} %cv_hbm.1, bf16[2,32,2048]{2,1,0:T(8,128)(2,1)} %dk_hbm.1, bf16[2,32,2048]{2,1,0:T(8,128)(2,1)} %dv_hbm.1, s32[2,64]{1,0:T(2,128)} %par_ref.1, s32[2]{0:T(128)} %len_ref.1, ...), custom_call_target="tpu_custom_call" | custom-call | tf_op jit(solution)/shard_map/pallas_call | solution.py:417
  44.5 1.9 %copy.10 = bf16[2,32,4096]{2,1,0:T(8,128)(2,1)} copy(bf16[2,32,4096]{2,1,0:T(8,128)(2,1)} %shard_map.82) | data formatting | bytes 1048576

commit v2 on v1

--- a/solution.py
+++ b/solution.py
@@ -17,7 +17,7 @@
 ORDER = ((0, 1), (1, 1), (0, 2), (0, 3), (1, 2), (1, 3), )
 STEPS = ((0, 1), (1, 1), (0, 2), (0, 3), (1, 2), (1, 3), )
 PASSED = (0, 1, )
-SCHEDULE = ("a00", "w", "w", "a01", "e0", "w", "w", "a10", "a11", "e1", "w", "w", "m0", "a20", "a21", "e2", "m1", "w", "a30", "a31", "e3", "w", "m2", "z0", "w", "m3", "w", "f0", "z1", "w", "w", "w", "f1", "z2", "w", "z3", "p00", "p01", "p10", "p11",)
+SCHEDULE = ("a00", "a01", "w", "w", "e0", "a10", "a11", "w", "w", "e1", "w", "w", "m0", "a20", "a21", "e2", "m1", "w", "a30", "a31", "e3", "w", "m2", "z0", "w", "m3", "w", "z1", "w", "w", "f0", "z2", "w", "f1", "w", "z3", "p00", "p01", "p10", "p11",)
 MESH = pl.DeviceIdType.MESH
 NEG = -1e30
 COEF = HEAD**-0.5 * 1.4426950408889634
@@ -190,13 +190,15 @@
         lax.broadcasted_iota(jnp.int32, (tree, own), 0)
         == lax.broadcasted_iota(jnp.int32, (tree, own), 1) + blk * own
     ).astype(jnp.float32).astype(jnp.bfloat16)
+    links = [
+        ((par_ref[pl.ds(r, 1), :] == row_i) | (row_i == col_i)).astype(jnp.float32) for r in range(batch)
+    ]
+    for _ in range((tree - 1).bit_length()):
+        links = [half.astype(jnp.bfloat16) for half in links]
+        links = [jnp.minimum(jnp.dot(half, half, preferred_element_type=jnp.float32), 1.0) for half in links]
     for r in range(batch):
-        links = ((par_ref[pl.ds(r, 1), :] == row_i) | (row_i == col_i)).astype(jnp.float32)
-        for _ in range((tree - 1).bit_length()):
-            half = links.astype(jnp.bfloat16)
-            links = jnp.minimum(jnp.dot(half, half, preferred_element_type=jnp.float32), 1.0)
         vtmp[r] = lax.dot_general(
-            links.astype(jnp.bfloat16), pick, (((0,), (0,)), ((), ())),
+            links[r].astype(jnp.bfloat16), pick, (((0,), (0,)), ((), ())),
             preferred_element_type=jnp.float32,
         )
     for r in range(batch):
@@ -263,12 +265,13 @@
             head(p, i)
 
     def exchange(p):
-        ssend[p] = stat[p].T[: 2 * per_p]
         for b in range(1, nblk):
             send(
                 nsend.at[:, :, pcols[p]], nrecv.at[back(b), :, :, pcols[p]],
                 n_send.at[p, b], n_recv.at[p, back(b)], member(0, 0, b),
             )
+        ssend[p] = stat[p].T[: 2 * per_p]
+        for b in range(1, nblk):
             send(ssend.at[p], srecv.at[p, back(b)], s_send.at[p, b], s_recv.at[p, back(b)], member(0, 0, b))
 
     def piece(zr, cr, yr, p):

time: 46.5 us -> 46.3 us (level)
  no operation moved by 1% of the time
where the time goes in v2:
time: 46.3 us; the launch traced here: 46.1 us
  Pallas kernels  44.2 us (95%)
  local copies, waits for them, and re-layouts  1.87 us (4%)
    pallas_call x1, Pallas kernels, shards(): pl.pallas_call(functools.partial(kernel, nreq, nblk), out_shape=jax.Shape...  44.2 us
    unnamed x1, local copies, waits for them, and re-layouts  1.87 us

profile of v2, /device:TPU:1, one launch (start us, length us, event | category | flops | bytes accessed | tf_op | source)
XLA Modules:
  0.0 46.1 jit_solution(10980657058276937385)
XLA Ops:
  0.0 44.2 %shard_map.82 = bf16[2,32,4096]{2,1,0:T(8,128)(2,1)} custom-call(bf16[2,32,2048]{2,1,0:T(8,128)(2,1)} %q_hbm.1, bf16[2,512,2048]{2,1,0:T(8,128)(2,1)} %ck_hbm.1, bf16[2,512,2048]{2,1,0:T(8,128)(2,1)} %cv_hbm.1, bf16[2,32,2048]{2,1,0:T(8,128)(2,1)} %dk_hbm.1, bf16[2,32,2048]{2,1,0:T(8,128)(2,1)} %dv_hbm.1, s32[2,64]{1,0:T(2,128)} %par_ref.1, s32[2]{0:T(128)} %len_ref.1, ...), custom_call_target="tpu_custom_call" | custom-call | tf_op jit(solution)/shard_map/pallas_call | solution.py:420
  44.3 1.9 %copy.10 = bf16[2,32,4096]{2,1,0:T(8,128)(2,1)} copy(bf16[2,32,4096]{2,1,0:T(8,128)(2,1)} %shard_map.82) | data formatting | bytes 1048576

commit v3 on v2

--- a/solution.py
+++ b/solution.py
@@ -308,17 +308,21 @@
                 abuf[b, :, cols] = row.astype(jnp.bfloat16)
             if b == 0 and p in PASSED:
                 share(p, (0, 0, 0), (1, 0, 0), (1, 0, 0), 0)
+            if p not in PASSED:
+                share(p, (0, 0, b), (1, 0, b), (1, 0, 0), 2 + 2 * nblk + b)
+        share(p, (0, 0, None), (0, 1, None), (0, 1, 0), 1)
+
+    def near(p):
         if p not in PASSED:
-            share(p, (0, 0, None), (1, 0, None), (1, 0, 0), 0)
-        share(p, (0, 0, None), (0, 1, None), (0, 1, 0), 1)
-
-    def near(p):
-        yr = 0 if p in PASSED else None
-        await_recv(piece(1, 0, yr, p), sem(1, 0, yr, p))
+            for b in range(nblk):
+                await_recv(piece(1, 0, b, p), sem(1, 0, b, p))
+                share(p, (1, 0, b), (1, 1, b), (0, 1, 0), 2 + 3 * nblk + b)
+            return
+        await_recv(piece(1, 0, 0, p), sem(1, 0, 0, p))
         if p in PASSED:
             for b in range(1, nblk):
                 share(p, (1, 0, 0), (1, 0, back(b)), (0, 0, b), 2 + b)
-        share(p, (1, 0, yr), (1, 1, yr), (0, 1, 0), 2)
+        share(p, (1, 0, 0), (1, 1, 0), (0, 1, 0), 2)
 
     def far(p):
         if p in PASSED:
@@ -368,7 +372,7 @@
                     await_recv(wdst(n, source), w_recv.at[n, source])
         if n == 0:
             for p in range(PARTS):
-                for yr in range(nblk) if zr and p in PASSED else (None,):
+                for yr in range(nblk) if zr else (None,):
                     await_recv(piece(zr, 1, yr, p), sem(zr, 1, yr, p))
         project(n, zr)
 

time: 46.3 us -> 46.3 us (level)
  no operation moved by 1% of the time
where the time goes in v3:
time: 46.3 us; the launch traced here: 46.1 us
  Pallas kernels  44.2 us (95%)
  local copies, waits for them, and re-layouts  1.87 us (4%)
    pallas_call x1, Pallas kernels, shards(): pl.pallas_call(functools.partial(kernel, nreq, nblk), out_shape=jax.Shape...  44.2 us
    unnamed x1, local copies, waits for them, and re-layouts  1.87 us

profile of v3, /device:TPU:1, one launch (start us, length us, event | category | flops | bytes accessed | tf_op | source)
XLA Modules:
  0.0 46.1 jit_solution(6789512494265747649)
XLA Ops:
  0.0 44.2 %shard_map.82 = bf16[2,32,4096]{2,1,0:T(8,128)(2,1)} custom-call(bf16[2,32,2048]{2,1,0:T(8,128)(2,1)} %q_hbm.1, bf16[2,512,2048]{2,1,0:T(8,128)(2,1)} %ck_hbm.1, bf16[2,512,2048]{2,1,0:T(8,128)(2,1)} %cv_hbm.1, bf16[2,32,2048]{2,1,0:T(8,128)(2,1)} %dk_hbm.1, bf16[2,32,2048]{2,1,0:T(8,128)(2,1)} %dv_hbm.1, s32[2,64]{1,0:T(2,128)} %par_ref.1, s32[2]{0:T(128)} %len_ref.1, ...), custom_call_target="tpu_custom_call" | custom-call | tf_op jit(solution)/shard_map/pallas_call | solution.py:424
  44.2 1.9 %copy.10 = bf16[2,32,4096]{2,1,0:T(8,128)(2,1)} copy(bf16[2,32,4096]{2,1,0:T(8,128)(2,1)} %shard_map.82) | data formatting | bytes 1048576
